TPU v7x, 256 devices: a whole 4x4x8 slice. The times are simulated.
256 devices in a mesh: dp: 16 (over x, y_hi, core), expert: 16 (over y_lo, z).
Axes of the slice: x: 4, y: 4 (y_hi: 2, y_lo: 2; y = y_hi * 2 + y_lo), z: 8, core: 2. Of those that a mesh axis runs over, the one named last changes fastest.
Arguments:
- tokens: bfloat16 [32768, 1024], P(('dp', 'expert')), may hold values from -6 to 6
- expert_ids: int32 [32768, 8], P(('dp', 'expert')), may hold values from 0 to 63, all different within a row; in each aligned block of 128 rows (0 to 127, 128 to 255, ...) at most 24 rows name the same one
- upstream: bfloat16 [32768, 1024], P(('dp', 'expert')), may hold values from -6 to 6
- router_weight: bfloat16 [1024, 64], replicated, may hold values from -0.1875 to 0.1875
- gate_matrix: bfloat16 [64, 384, 1024], P('expert'), may hold values from -0.1875 to 0.1875
- up_matrix: bfloat16 [64, 384, 1024], P('expert'), may hold values from -0.1875 to 0.1875
- down_matrix: bfloat16 [64, 384, 1024], P('expert'), may hold values from -0.3125 to 0.3125
Outputs:
- mixture: bfloat16 [32768, 1024], P(('dp', 'expert'))
- input_grad: bfloat16 [32768, 1024], P(('dp', 'expert'))
- router_grad: float32 [1024, 64], replicated
- gate_grad: float32 [64, 384, 1024], P('expert', 'dp')
- up_grad: float32 [64, 384, 1024], P('expert', 'dp')
- down_grad: float32 [64, 384, 1024], P('expert', 'dp')
Inputs may be any that keep to these rules, and one draw needn't show every extreme that they name: `expert_ids`: each row names 8 different experts. Among the rows of one device no expert is named more than 24 times, a bound that some block reaches.
All inputs are finite; a program needn't handle non-finite values.
Results may differ from a plain program's by a relative error of at most 0.0063.
Values may be sent and summed in bfloat16 or wider, within the bound.
No kernel may reach another device: no remote copies, remote signals or barrier semaphores. Data moves between devices by JAX's collectives and lax.ppermute only.
A program may use at most 320 MiB of HBM per device.

v0:
```python
import jax
import jax.numpy as jnp
from jax import lax
from jax.sharding import PartitionSpec as P


def slot_positions(expert_ids, experts, capacity):
    flat_ids = expert_ids.reshape(-1)
    columns = lax.broadcasted_iota(jnp.int32, (1, experts), 1)
    onehot = (flat_ids[:, None] == columns).astype(jnp.int32)
    ranking = jnp.cumsum(onehot, axis=0) - 1
    slot_numbers = jnp.sum(ranking * onehot, axis=1)
    return flat_ids * capacity + slot_numbers


def slot_sources(positions, total_slots):
    assign_count = positions.shape[0]
    return (
        jnp.full((total_slots,), -1, jnp.int32)
        .at[positions]
        .set(jnp.arange(assign_count, dtype=jnp.int32))
    )


def fill_slots(source_rows, sources, divisor):
    occupied = sources >= 0
    picked = jnp.take(source_rows, jnp.maximum(sources, 0) // divisor, axis=0)
    return jnp.where(occupied[:, None], picked, jnp.zeros_like(picked))


def backward_local(pre_gate, pre_up, logistic, act_grad):
    gate_back = (act_grad * pre_up * logistic * (1.0 + pre_gate * (1.0 - logistic))).astype(
        jnp.bfloat16
    )
    up_back = (act_grad * (pre_gate * logistic)).astype(jnp.bfloat16)
    return (gate_back, up_back)


def body(tokens, expert_ids, upstream, router_weight, gate_matrix, up_matrix, down_matrix):
    tok_rows, model_width = tokens.shape
    per_token = expert_ids.shape[1]
    exp_dev, hidden = (gate_matrix.shape[0], gate_matrix.shape[1])
    expert_peers = lax.axis_size("expert")
    experts = expert_peers * exp_dev
    capacity = tok_rows * per_token * 3 // (2 * experts)
    positions = slot_positions(expert_ids, experts, capacity)
    sources = slot_sources(positions, experts * capacity)
    send_rows = fill_slots(tokens, sources, per_token).reshape(
        expert_peers, exp_dev * capacity, model_width
    )
    recv_rows = lax.all_to_all(send_rows, "expert", split_axis=0, concat_axis=0, tiled=True)
    expert_rows = recv_rows.reshape(expert_peers, exp_dev, capacity, model_width)
    pre_gate = jnp.einsum(
        "secd,efd->secf", expert_rows, gate_matrix, preferred_element_type=jnp.float32
    )
    pre_up = jnp.einsum(
        "secd,efd->secf", expert_rows, up_matrix, preferred_element_type=jnp.float32
    )
    logistic = jax.nn.sigmoid(pre_gate)
    activated = (pre_gate * logistic * pre_up).astype(jnp.bfloat16)
    produced = jnp.einsum(
        "secf,efd->secd", activated, down_matrix, preferred_element_type=jnp.float32
    ).astype(jnp.bfloat16)
    returned = lax.all_to_all(
        produced.reshape(expert_peers, exp_dev * capacity, model_width),
        "expert",
        split_axis=0,
        concat_axis=0,
        tiled=True,
    )
    assign_out = jnp.take(returned.reshape(experts * capacity, model_width), positions, axis=0)
    assign_out = assign_out.reshape(tok_rows, per_token, model_width).astype(jnp.float32)
    logits = jnp.dot(tokens, router_weight, preferred_element_type=jnp.float32)
    chosen = jnp.take_along_axis(logits, expert_ids, axis=1)
    raised = jnp.exp(chosen)
    gate_probs = raised / jnp.sum(raised, axis=1, keepdims=True)
    mixture = jnp.sum(gate_probs[:, :, None] * assign_out, axis=1).astype(jnp.bfloat16)
    cotangent = upstream.astype(jnp.float32)
    prob_grad = jnp.sum(cotangent[:, None, :] * assign_out, axis=2)
    centered = prob_grad - jnp.sum(gate_probs * prob_grad, axis=1, keepdims=True)
    chosen_grad = gate_probs * centered
    expert_cols = lax.broadcasted_iota(jnp.int32, (1, 1, experts), 2)
    logit_grad = jnp.sum(
        jnp.where(expert_ids[:, :, None] == expert_cols, chosen_grad[:, :, None], 0.0), axis=1
    )
    router_part = jnp.dot(tokens.astype(jnp.float32).T, logit_grad, precision=lax.Precision.HIGHEST)
    router_grad = lax.psum(router_part, ("dp", "expert"))
    router_input = jnp.dot(
        logit_grad, router_weight.astype(jnp.float32).T, precision=lax.Precision.HIGHEST
    )
    out_grad = (gate_probs[:, :, None] * cotangent[:, None, :]).astype(jnp.bfloat16)
    out_grad = out_grad.reshape(tok_rows * per_token, model_width)
    send_grad = fill_slots(out_grad, sources, 1).reshape(
        expert_peers, exp_dev * capacity, model_width
    )
    recv_grad = lax.all_to_all(send_grad, "expert", split_axis=0, concat_axis=0, tiled=True)
    grad_rows = recv_grad.reshape(expert_peers, exp_dev, capacity, model_width)
    act_grad = jnp.einsum(
        "secd,efd->secf", grad_rows, down_matrix, preferred_element_type=jnp.float32
    )
    gate_back, up_back = backward_local(pre_gate, pre_up, logistic, act_grad)
    row_grad = (
        jnp.einsum("secf,efd->secd", gate_back, gate_matrix, preferred_element_type=jnp.float32)
        + jnp.einsum("secf,efd->secd", up_back, up_matrix, preferred_element_type=jnp.float32)
    ).astype(jnp.bfloat16)
    returned_grads = lax.all_to_all(
        row_grad.reshape(expert_peers, exp_dev * capacity, model_width),
        "expert",
        split_axis=0,
        concat_axis=0,
        tiled=True,
    )
    per_assign = jnp.take(
        returned_grads.reshape(experts * capacity, model_width), positions, axis=0
    )
    per_assign = per_assign.reshape(tok_rows, per_token, model_width).astype(jnp.float32)
    input_grad = (jnp.sum(per_assign, axis=1) + router_input).astype(jnp.bfloat16)
    full_gate = jnp.einsum(
        "secf,secd->efd", gate_back, expert_rows, preferred_element_type=jnp.float32
    )
    full_up = jnp.einsum("secf,secd->efd", up_back, expert_rows, preferred_element_type=jnp.float32)
    full_down = jnp.einsum(
        "secf,secd->efd", activated, grad_rows, preferred_element_type=jnp.float32
    )
    gate_grad = lax.psum_scatter(full_gate, "dp", scatter_dimension=1, tiled=True)
    up_grad = lax.psum_scatter(full_up, "dp", scatter_dimension=1, tiled=True)
    down_grad = lax.psum_scatter(full_down, "dp", scatter_dimension=1, tiled=True)
    return (mixture, input_grad, router_grad, gate_grad, up_grad, down_grad)


def solution(mesh):
    in_specs = (
        P(("dp", "expert"), None),
        P(("dp", "expert"), None),
        P(("dp", "expert"), None),
        P(),
        P("expert", None, None),
        P("expert", None, None),
        P("expert", None, None),
    )
    out_specs = (
        P(("dp", "expert"), None),
        P(("dp", "expert"), None),
        P(),
        P("expert", "dp", None),
        P("expert", "dp", None),
        P("expert", "dp", None),
    )
    return jax.shard_map(body, mesh=mesh, in_specs=in_specs, out_specs=out_specs, check_vma=False)
```

profile of v0, /device:TPU:2, one launch (start us, length us, event | category | flops | bytes accessed | tf_op | source)
XLA Modules:
  0.0 670.4 jit_solution(13618022292784977458)
XLA Ops:
  10.9 34.2 %reduce-window.6 = s32[64,8,128]{2,1,0:T(8,128)} reduce-window(s32[64,8,128]{2,1,0:T(8,128)} %fusion.43, s32[]{:T(128)} %constant.85.clone.1), window={size=1x1x128 pad=0_0x0_0x127_0}, to_apply=%region_1.2 | reduce-window | flops 8323072 | bytes 524292 | tf_op jit(solution)/shard_map/reduce-window
  45.1 1.8 slice.18
  49.3 4.3 scatter_custom_fusion
  53.8 5.8 gather_fusion
  59.7 2.2 select_select_fusion.1
  61.9 81.5 %all_to_all.20 = bf16[16,96,1024]{2,1,0:T(8,128)(2,1)S(1)} all-to-all(bf16[16,96,1024]{2,1,0:T(8,128)(2,1)S(1)} %select_select_fusion.1), channel_id=1, replica_groups=mesh['dp'=16,'expert'=16] {'expert'}, dimensions={0} | all-to-all | bytes 6291456 | tf_op jit(solution)/shard_map/all_to_all | solution.py:51
  143.4 1.9 fusion.11
  146.4 3.5 fusion.27
  149.9 1.8 convert_bitcast_fusion.1
  151.7 2.1 copy.64
  153.9 4.8 all-to-all-start.1
  160.0 7.0 %gather_fusion.2 = f32[1024]{0:T(1024)S(1)} fusion(f32[128,64]{0,1:T(8,128)S(1)} %fusion.48, s32[1024]{0:T(1024)S(1)} %reshape.214), kind=kCustom, calls=%fused_computation.4 | custom fusion | bytes 16384 | tf_op jit(solution)/shard_map/jit(take_along_axis)/gather | solution.py:74
  167.3 1.8 convert_element_type.63
  169.2 61.6 %all-to-all-done.1 = bf16[16,96,1024]{2,1,0:T(8,128)(2,1)} async-done(((bf16[16,96,1024]{2,1,0:T(8,128)(2,1)}), bf16[16,96,1024]{2,1,0:T(8,128)(2,1)}, u32[]{:S(2)}, u32[]{:S(2)}) %all-to-all-start.1) | async-done | bytes 3145760 | tf_op jit(solution)/shard_map/all_to_all | solution.py:64
  230.8 8.3 %gather_fusion.3 = bf16[1024,1024]{1,0:T(8,128)(2,1)} fusion(bf16[1536,1024]{1,0:T(8,128)(2,1)} %bitcast.17, s32[1024]{0:T(1024)S(1)} %broadcast_clamp_fusion), kind=kCustom, calls=%fused_computation.clone | custom fusion | bytes 4198400 | tf_op jit(solution)/shard_map/jit(_take)/gather | solution.py:71
  239.2 2.5 fusion.3
  242.1 2.7 fusion.2
  244.8 9.6 %gather_fusion.1 = bf16[1536,1024]{1,0:T(8,128)(2,1)} fusion(bf16[1024,1024]{1,0:T(8,128)(2,1)} %fusion.2, s32[2048]{0:T(1024)S(1)} %pad_clamp_fusion), kind=kCustom, calls=%fused_computation.3 | custom fusion | bytes 6297600 | tf_op jit(solution)/shard_map/jit(_take)/gather | solution.py:27
  254.4 3.4 select_select_fusion
  257.8 7.5 %all-to-all-start.2 = ((bf16[16,96,1024]{2,1,0:T(8,128)(2,1)}), bf16[16,96,1024]{2,1,0:T(8,128)(2,1)}, u32[]{:S(2)}, u32[]{:S(2)}) async-start(bf16[16,96,1024]{2,1,0:T(8,128)(2,1)} %select_select_fusion), calls=%async_computation.2 | async-start | bytes 6291456 | tf_op jit(solution)/shard_map/all_to_all | solution.py:96
  266.4 69.4 %all-to-all-done.2 = bf16[16,96,1024]{2,1,0:T(8,128)(2,1)} async-done(((bf16[16,96,1024]{2,1,0:T(8,128)(2,1)}), bf16[16,96,1024]{2,1,0:T(8,128)(2,1)}, u32[]{:S(2)}, u32[]{:S(2)}) %all-to-all-start.2) | async-done | bytes 3145760 | tf_op jit(solution)/shard_map/all_to_all | solution.py:96
  335.8 6.8 %fusion.20 = f32[4,384,1024]{2,1,0:T(8,128)} fusion(bf16[16,4,24,384]{3,2,0,1:T(8,128)(2,1)} %copy-done.7, bf16[16,4,24,1024]{3,2,1,0:T(8,128)(2,1)} %bitcast.21), kind=kOutput, calls=%fused_computation.34 | convolution fusion | flops 1207959552 | bytes 10616832 | tf_op jit(solution)/shard_map/secf,secd->efd/dot_general | solution.py:122
  342.7 6.8 %fusion.25 = (bf16[16,4,24,384]{3,2,0,1:T(8,128)(2,1)S(1)}, bf16[16,4,24,384]{3,2,0,1:T(8,128)(2,1)}) fusion(f32[4,16,24,384]{3,2,1,0:T(8,128)} %get-tuple-element.18, f32[4,16,24,384]{3,2,1,0:T(8,128)} %copy-done.12, bf16[4,384,1024]{2,1,0:T(8,128)(2,1)S(1)} %copy-done, bf16[16,4,24,1024]{3,2,1,0:T(8,128)(2,1)} %bitcast.21), kind=kOutput, calls=%fused_computation.41 | convolution fusion | flops 1215627264 | bytes 13369344 | tf_op jit(solution)/shard_map/secd,efd->secf/dot_general | solution.py:98
  350.6 4.5 convolution_bitcast_fusion.1
  355.4 6.8 %convolution_bitcast_fusion = f32[4,384,1024]{2,1,0:T(8,128)} fusion(bf16[16,4,24,384]{3,2,0,1:T(8,128)(2,1)} %get-tuple-element.14, bf16[16,4,24,1024]{3,2,1,0:T(8,128)(2,1)} %bitcast.146), kind=kOutput, calls=%fused_computation.35 | convolution fusion | flops 1207959552 | bytes 10616832 | tf_op jit(solution)/shard_map/secf,secd->efd/dot_general | solution.py:121
  362.2 4.5 fusion.5
  366.8 1.8 fusion.4
  368.9 81.1 %all_to_all.21 = bf16[16,96,1024]{2,1,0:T(8,128)(2,1)} all-to-all(bf16[16,96,1024]{2,1,0:T(8,128)(2,1)S(1)} %bitcast.141), channel_id=1, replica_groups=mesh['dp'=16,'expert'=16] {'expert'}, dimensions={0} | all-to-all | bytes 6291456 | tf_op jit(solution)/shard_map/all_to_all | solution.py:106
  450.0 8.4 %gather_fusion.4 = bf16[1024,1024]{1,0:T(8,128)(2,1)} fusion(bf16[1536,1024]{1,0:T(8,128)(2,1)} %bitcast.139, s32[1024]{0:T(1024)S(1)} %broadcast_clamp_fusion), kind=kCustom, calls=%fused_computation.1.clone | custom fusion | bytes 4198400 | tf_op jit(solution)/shard_map/jit(_take)/gather | solution.py:113
  458.3 5.2 convert_reduce_fusion
  464.7 101.7 %all-reduce.2.cloned.1.call-done = f32[1024,64]{0,1:T(8,128)} async-done(((f32[1024,64]{0,1:T(8,128)}), f32[1024,64]{0,1:T(8,128)}) %all-reduce.2.cloned.1.call-update) | async-done | bytes 262160 | tf_op jit(solution)/shard_map/psum | solution.py:87
  566.4 94.6 %reduce-scatter.6.cloned.1.call-done = f32[4,24,1024]{2,1,0:T(8,128)} async-done(((f32[4,384,1024]{2,1,0:T(8,128)}), f32[4,24,1024]{2,1,0:T(8,128)}) %reduce-scatter.6.cloned.1.call-update) | async-done | bytes 393232 | tf_op jit(solution)/shard_map/reduce_scatter | solution.py:126
  (78 shorter events, 14.3 us)
Async XLA Ops:
  8.0 141.9 %copy-start = (bf16[4,384,1024]{2,1,0:T(8,128)(2,1)S(1)}, bf16[4,384,1024]{2,1,0:T(8,128)(2,1)}, u32[]{:S(2)}) copy-start(bf16[4,384,1024]{2,1,0:T(8,128)(2,1)} %param.15) | copy-start | bytes 9437188
  8.0 45.8 %copy-start.1 = (bf16[128,1024]{1,0:T(8,128)(2,1)S(1)}, bf16[128,1024]{1,0:T(8,128)(2,1)}, u32[]{:S(2)}) copy-start(bf16[128,1024]{1,0:T(8,128)(2,1)} %param.9) | copy-start | bytes 786436
  61.8 81.5 %copy-start.4 = (bf16[4,384,1024]{2,1,0:T(8,128)(2,1)S(1)}, bf16[4,384,1024]{2,1,0:T(8,128)(2,1)}, u32[]{:S(2)}) copy-start(bf16[4,384,1024]{2,1,0:T(8,128)(2,1)} %param.13) | copy-start | bytes 9437188
  143.4 1.9 copy-start.2
  143.4 3.0 copy-start.6
  146.4 3.5 copy-start.12
  149.9 1.8 copy-start.7
  153.9 4.8 copy-start.11
  153.9 76.9 %all-to-all-start.1 = ((bf16[16,96,1024]{2,1,0:T(8,128)(2,1)}), bf16[16,96,1024]{2,1,0:T(8,128)(2,1)}, u32[]{:S(2)}, u32[]{:S(2)}) async-start(bf16[16,96,1024]{2,1,0:T(8,128)(2,1)} %bitcast.140), calls=%async_computation.1 | async-start | bytes 6291456 | tf_op jit(solution)/shard_map/all_to_all | solution.py:64
  257.8 78.0 %all-to-all-start.2 = ((bf16[16,96,1024]{2,1,0:T(8,128)(2,1)}), bf16[16,96,1024]{2,1,0:T(8,128)(2,1)}, u32[]{:S(2)}, u32[]{:S(2)}) async-start(bf16[16,96,1024]{2,1,0:T(8,128)(2,1)} %select_select_fusion), calls=%async_computation.2 | async-start | bytes 6291456 | tf_op jit(solution)/shard_map/all_to_all | solution.py:96
  265.2 301.2 %all-reduce.2.cloned.1.call-start = ((), (), s32[]{:S(2)}) async-start(), calls=%async_computation.7 | async-start | bytes 524288 | tf_op jit(solution)/shard_map/psum | solution.py:87
  266.3 300.1 %reduce-scatter.8.cloned.1.call-start = ((), (), s32[]{:S(2)}) async-start(), calls=%async_computation.10 | async-start | bytes 6684672 | tf_op jit(solution)/shard_map/reduce_scatter | solution.py:127
  342.6 223.9 %reduce-scatter.4.cloned.1.call-start = ((), (), s32[]{:S(2)}) async-start(), calls=%async_computation.8 | async-start | bytes 6684672 | tf_op jit(solution)/shard_map/reduce_scatter | solution.py:125
  342.6 7.9 %copy-start.3 = (bf16[16,96,1024]{2,1,0:T(8,128)(2,1)S(1)}, bf16[16,96,1024]{2,1,0:T(8,128)(2,1)}, u32[]{:S(2)}) copy-start(bf16[16,96,1024]{2,1,0:T(8,128)(2,1)} %copy-done.2) | copy-start | bytes 9437188
  349.5 1.1 copy-start.8
  355.1 306.0 %reduce-scatter.6.cloned.1.call-start = ((), (), s32[]{:S(2)}) async-start(), calls=%async_computation.9 | async-start | bytes 6684672 | tf_op jit(solution)/shard_map/reduce_scatter | solution.py:126
  362.2 4.6 copy-start.5
  362.2 4.6 copy-start.9
  458.3 5.2 copy-start.10
Sparse Core Ops, SparseCore 0:
  272.1 294.2 all-reduce.1
Sparse Core Ops, SparseCore 1:
  342.7 116.4 reduce-scatter.7
  464.0 96.0 reduce-scatter.3
  565.0 96.1 reduce-scatter.5
where the time goes:
time: 673 us; the launch traced here: 670 us
  waiting for transfers between devices  327 us (49%)
  blocking collectives  163 us (24%)
  local copies, waits for them, and re-layouts  55.1 us (8%)
  other arithmetic  54.9 us (8%)
  matrix products  41.6 us (6%)
  between operations  16 us (2%)
  starting transfers between devices  12.7 us (2%)
    psum x1, waiting for transfers between devices, body(): router_grad = lax.psum(router_part, ('dp', 'expert'))  102 us
    reduce_scatter x1, waiting for transfers between devices, body(): up_grad = lax.psum_scatter(full_up, 'dp', scatter_dimension=1, tiled=True)  94.6 us
    all_to_all x1, blocking collectives, body(): lax.all_to_all(send_rows, 'expert', split_axis=0, concat_axis=0, tiled=True)  81.5 us
    all_to_all x1, blocking collectives, body(): lax.all_to_all(row_grad.reshape(expert_peers, exp_dev * capacity, model_w...  81.1 us
    all_to_all x1, waiting for transfers between devices, body(): lax.all_to_all(send_grad, 'expert', split_axis=0, concat_axis=0, tiled=True)  69.4 us
    all_to_all x1, waiting for transfers between devices, body(): lax.all_to_all(produced.reshape(expert_peers, exp_dev * capacity, model_w...  61.6 us
    another operation x2, other arithmetic  34.2 us
    gather x2, local copies, waits for them, and re-layouts, fill_slots(): picked = jnp.take(source_rows, jnp.maximum(sources, 0) // divisor, axis=0)  15.5 us
  transfers between devices with their start and end apart: 6, of which 4 were waited for; matrix products, arithmetic and copies ran while one was open for 9% of the time, Pallas kernels for 0%

commit v1 on v0

v1 whole, which is shorter than its diff:
```python
import functools

import jax
import jax.numpy as jnp
from jax import lax
from jax.experimental import pallas as pl
from jax.experimental.pallas import tpu as pltpu
from jax.sharding import PartitionSpec as P

BF = jnp.bfloat16
F32 = jnp.float32
EXPERT = ("yl", "z")
DP = ("x", "yh", "core")
ALL = DP + EXPERT


def nt(a, b):
    return lax.dot_general(a, b, (((1,), (1,)), ((), ())), preferred_element_type=F32)


def tn(a, b):
    return lax.dot_general(a, b, (((0,), (0,)), ((), ())), preferred_element_type=F32)


def nn(a, b):
    return jnp.dot(a, b, preferred_element_type=F32)


def pack_kernel(tokens, ids, upstream, router, payload):
    rows = tokens.shape[0]
    experts = router.shape[0]
    payload[0:rows] = tokens[...]
    payload[rows : 2 * rows] = upstream[...]
    logits = nt(router[...], tokens[...])
    names = lax.broadcasted_iota(jnp.int32, (experts, rows), 0)
    chosen = names == ids[0:1, :]
    for k in range(1, ids.shape[0]):
        chosen = chosen | (names == ids[k : k + 1, :])
    raised = jnp.where(chosen, jnp.exp(logits), 0.0)
    probs = raised / jnp.sum(raised, axis=0, keepdims=True)
    wide = jnp.concatenate([probs[8 * b : 8 * b + 8, :] for b in range(experts // 8)], axis=1)
    high = wide.astype(BF).astype(F32)
    payload[2 * rows : 2 * rows + 16] = jnp.concatenate([high, wide - high], axis=0).astype(BF)


def expert_kernel(
    first,
    payload,
    gate,
    up,
    down,
    router,
    out,
    grads,
    router_part,
    x_rows,
    u_rows,
    picks,
    spreads,
    probs,
    local,
    weight,
    scores,
    produced,
    row_grads,
    down_kept,
    *,
    cap,
):
    e = pl.program_id(0)
    sources, _, width = payload.shape
    mine = local.shape[1]
    pairs, slots, pair_rows = picks.shape
    rows = pair_rows // 2
    experts = router.shape[0]
    two = 2 * cap
    at_first = first[0]

    def pair_of(p, start):
        return jnp.concatenate(
            [payload[2 * p, start : start + rows], payload[2 * p + 1, start : start + rows]], axis=0
        )

    @pl.when(e == 0)
    def _():
        t_from = lax.broadcasted_iota(jnp.int32, (rows, rows), 0)
        t_to = lax.broadcasted_iota(jnp.int32, (rows, rows), 1)
        before = jnp.where(t_from < t_to, 1.0, 0.0).astype(BF)
        names = lax.broadcasted_iota(jnp.int32, (experts, pair_rows), 0)
        slot_down = lax.broadcasted_iota(jnp.int32, (two, pair_rows), 0).astype(F32)
        slot_across = lax.broadcasted_iota(jnp.int32, (pair_rows, slots), 1).astype(F32)

        @pl.loop(0, pairs)
        def _(p):
            halves = []
            for h in range(2):
                ext = payload[2 * p + h, 2 * rows : 2 * rows + 16].astype(F32)
                wide = ext[0:8] + ext[8:16]
                halves.append(
                    jnp.concatenate(
                        [wide[:, rows * b : rows * b + rows] for b in range(experts // 8)], axis=0
                    )
                )
            all_probs = jnp.concatenate(halves, axis=1)
            probs[p] = all_probs
            own = [
                jnp.sum(jnp.where(names == at_first + j, all_probs, 0.0), axis=0, keepdims=True)
                for j in range(mine)
            ]
            own = jnp.concatenate(own + [jnp.zeros((8 - mine, pair_rows), F32)], axis=0)
            local[p] = own[0:mine]
            taken = jnp.where(own > 0.0, 1.0, 0.0)
            rank = jnp.concatenate(
                [
                    nn(taken[:, 0:rows].astype(BF), before),
                    nn(taken[:, rows:].astype(BF), before) + float(cap),
                ],
                axis=1,
            )
            slot = jnp.where(taken > 0.0, rank, -1000.0)
            parts = []
            for j in range(mine):
                hit = slot_down == slot[j : j + 1, :]
                parts.append(jnp.where(hit, 1.0, 0.0))
                weight[j, pl.ds(pl.multiple_of(p * two, two), two), :] = jnp.sum(
                    jnp.where(hit, own[j : j + 1, :], 0.0), axis=1, keepdims=True
                )
            pick = jnp.concatenate(parts, axis=0).astype(BF)
            picks[p] = pick
            slot_t = jnp.transpose(slot)
            spread = jnp.zeros((pair_rows, slots), F32)
            for j in range(mine):
                spread = jnp.where(
                    slot_across == slot_t[:, j : j + 1] + float(j * two),
                    jnp.where(slot_t[:, j : j + 1] >= 0.0, 1.0, 0.0), spread
                )
            spreads[p] = spread.astype(BF)
            here = pl.ds(pl.multiple_of(p * two, two), two)
            got = nn(pick, pair_of(p, 0)).astype(BF)
            for j in range(mine):
                x_rows[j, here, :] = got[j * two : j * two + two]
            got = nn(pick, pair_of(p, rows)).astype(BF)
            for j in range(mine):
                u_rows[j, here, :] = got[j * two : j * two + two]

    x = x_rows[e]
    u = u_rows[e]
    pre_gate = nt(x, gate[0])
    pre_up = nt(x, up[0])
    raw = nt(u, down[0])
    g = weight[e]
    logistic = jax.nn.sigmoid(pre_gate)
    swished = pre_gate * logistic
    activated = swished * pre_up
    scores[e] = jnp.sum(activated * raw, axis=1, keepdims=True)
    act_grad = raw * g
    scaled = (activated * g).astype(BF)
    gate_back = (act_grad * pre_up * logistic * (1.0 + pre_gate * (1.0 - logistic))).astype(BF)
    up_back = (act_grad * swished).astype(BF)
    at = pl.ds(pl.multiple_of(e * two, two), two)
    made = nn(scaled, down[0]).astype(BF)
    back = (nn(gate_back, gate[0]) + nn(up_back, up[0])).astype(BF)
    for p in range(pairs):
        produced[p, at, :] = made[p * two : p * two + two]
        row_grads[p, at, :] = back[p * two : p * two + two]
    chunks = grads.shape[0]
    gate_grad = tn(gate_back, x)
    up_grad = tn(up_back, x)
    piece = gate_grad.shape[0] // chunks
    for d in range(chunks):
        cut = slice(d * piece, d * piece + piece)
        grads[d, pl.ds(pl.multiple_of(e * 2 * piece, 2 * piece), 2 * piece), :] = jnp.concatenate(
            [gate_grad[cut], up_grad[cut]], axis=0
        ).astype(BF)
    down_grad = tn(scaled, u)

    @pl.when(e % 2 == 0)
    def _():
        down_kept[...] = down_grad

    @pl.when(e % 2 == 1)
    def _():
        base = mine * 2 * piece + (e // 2) * 2 * piece
        for d in range(chunks):
            cut = slice(d * piece, d * piece + piece)
            grads[d, pl.ds(pl.multiple_of(base, 2 * piece), 2 * piece), :] = jnp.concatenate(
                [down_kept[cut], down_grad[cut]], axis=0
            ).astype(BF)

    @pl.when(e == mine - 1)
    def _():
        names = lax.broadcasted_iota(jnp.int32, (experts, pair_rows), 0)
        router_part[...] = jnp.zeros_like(router_part)

        @pl.loop(0, pairs)
        def _(p):
            spread = spreads[p]
            mix = nn(spread, produced[p]).astype(BF)
            out[2 * p, 0:rows] = mix[0:rows]
            out[2 * p + 1, 0:rows] = mix[rows:]
            pick = picks[p].astype(F32)
            own = local[p]
            total = jnp.zeros((1, pair_rows), F32)
            placed = jnp.zeros((experts, pair_rows), F32)
            for j in range(mine):
                score = scores[j, pl.ds(pl.multiple_of(p * two, two), two), :]
                grad = own[j : j + 1] * jnp.sum(
                    pick[j * two : j * two + two] * score, axis=0, keepdims=True
                )
                total = total + grad
                placed = jnp.where(names == at_first + j, grad, placed)
            logit_grad = placed - probs[p] * total
            high = logit_grad.astype(BF)
            low = (logit_grad - high.astype(F32)).astype(BF)
            both = nn(jnp.concatenate([high, low], axis=0), pair_of(p, 0))
            router_part[...] += both[0:experts] + both[experts:]
            back = (nn(spread, row_grads[p]) + tn(high, router[...])).astype(BF)
            out[2 * p, rows : 2 * rows] = back[0:rows]
            out[2 * p + 1, rows : 2 * rows] = back[rows:]


def run_experts(first, payload, gate, up, down, router, cap, chunks):
    sources, payload_rows, width = payload.shape
    mine, hidden, _ = gate.shape
    experts = router.shape[0]
    rows = (payload_rows - 16) // 2
    pairs, slots, total = sources // 2, 2 * mine * cap, sources * cap
    whole = functools.partial(pl.BlockSpec, pipeline_mode=pl.Buffered(1))
    one = lambda: pl.BlockSpec((1, hidden, width), lambda e: (e, 0, 0))
    grad_rows = 3 * mine * hidden // chunks
    return pl.pallas_call(
        functools.partial(expert_kernel, cap=cap),
        grid=(mine,),
        out_shape=(
            jax.ShapeDtypeStruct((sources, 2 * rows, width), BF),
            jax.ShapeDtypeStruct((chunks, grad_rows, width), BF),
            jax.ShapeDtypeStruct((experts, width), F32),
        ),
        in_specs=[
            pl.BlockSpec(memory_space=pltpu.SMEM),
            whole((sources, payload_rows, width), lambda e: (0, 0, 0)),
            one(),
            one(),
            one(),
            whole((experts, width), lambda e: (0, 0)),
        ],
        out_specs=(
            whole((sources, 2 * rows, width), lambda e: (0, 0, 0)),
            whole((chunks, grad_rows, width), lambda e: (0, 0, 0)),
            whole((experts, width), lambda e: (0, 0)),
        ),
        scratch_shapes=[
            pltpu.VMEM((mine, total, width), BF),
            pltpu.VMEM((mine, total, width), BF),
            pltpu.VMEM((pairs, slots, 2 * rows), BF),
            pltpu.VMEM((pairs, 2 * rows, slots), BF),
            pltpu.VMEM((pairs, experts, 2 * rows), F32),
            pltpu.VMEM((pairs, mine, 2 * rows), F32),
            pltpu.VMEM((mine, total, 1), F32),
            pltpu.VMEM((mine, total, 1), F32),
            pltpu.VMEM((pairs, slots, width), BF),
            pltpu.VMEM((pairs, slots, width), BF),
            pltpu.VMEM((hidden, width), F32),
        ],
        compiler_params=pltpu.CompilerParams(vmem_limit_bytes=60 * 2**20),
        cost_estimate=pl.CostEstimate(
            flops=16 * 10**9, bytes_accessed=32 * 2**20, transcendentals=10**6
        ),
    )(first, payload, gate, up, down, router)


def body(tokens, expert_ids, upstream, router_weight, gate_matrix, up_matrix, down_matrix):
    rows, width = tokens.shape
    top = expert_ids.shape[1]
    mine, hidden, _ = gate_matrix.shape
    peers = lax.axis_size(EXPERT)
    groups = lax.axis_size(DP)
    experts = peers * mine
    cap = rows * top * 3 // (2 * experts)
    router = router_weight.T
    payload = pl.pallas_call(
        pack_kernel,
        out_shape=jax.ShapeDtypeStruct((2 * rows + 16, width), BF),
    )(tokens, expert_ids.T, upstream, router)
    gathered = lax.all_gather(payload, EXPERT, axis=0, tiled=False)
    first = (lax.axis_index(EXPERT) * mine).reshape(1).astype(jnp.int32)
    out, grads, router_part = run_experts(
        first, gathered, gate_matrix, up_matrix, down_matrix, router, cap, groups
    )
    router_grad = lax.psum(router_part, ALL).T
    grads = lax.psum_scatter(grads, DP, scatter_dimension=0, tiled=False)
    out = lax.psum_scatter(out, EXPERT, scatter_dimension=0, tiled=False)
    piece = hidden // groups
    both = grads[0 : 2 * mine * piece].astype(F32).reshape(mine, 2, piece, width)
    down_grad = grads[2 * mine * piece :].astype(F32).reshape(mine, piece, width)
    return out[0:rows], out[rows:], router_grad, both[:, 0], both[:, 1], down_grad


def solution(mesh):
    shape = {"x": 4, "yh": 2, "core": 2, "yl": 2, "z": 8}
    fine = jax.sharding.Mesh(mesh.devices.reshape(tuple(shape.values())), tuple(shape))
    in_specs = (
        P(ALL, None),
        P(ALL, None),
        P(ALL, None),
        P(),
        P(EXPERT, None, None),
        P(EXPERT, None, None),
        P(EXPERT, None, None),
    )
    out_specs = (
        P(ALL, None),
        P(ALL, None),
        P(),
        P(EXPERT, DP, None),
        P(EXPERT, DP, None),
        P(EXPERT, DP, None),
    )
    return jax.shard_map(body, mesh=fine, in_specs=in_specs, out_specs=out_specs, check_vma=False)
```

time: 673 us -> 634 us (0.942)
  waiting for transfers between devices: 327 us -> 573 us
  blocking collectives: 163 us -> 0 us
  other arithmetic: 54.9 us -> 0.86 us
  local copies, waits for them, and re-layouts: 55.1 us -> 6.41 us
  matrix products: 41.6 us -> 0 us
  Pallas kernels: 0 us -> 39.7 us
  starting transfers between devices: 12.7 us -> 0.16 us
    all_to_all x2 -> x0, blocking collectives: 163 us -> none  [the longest x1 81.5 us: body(): lax.all_to_all(send_rows, 'expert', split_axis=0, concat_axis=0, tiled=True)]
    psum x1, waiting for transfers between devices: 102 us -> 252 us  [body(): router_grad = lax.psum(router_part, ALL).T]
    all_to_all x2 -> x0, waiting for transfers between devices: 131 us -> none  [the longest x1 69.4 us: body(): lax.all_to_all(send_grad, 'expert', split_axis=0, concat_axis=0, tiled=True)]
    reduce_scatter x3 -> x2, waiting for transfers between devices: 94.7 us -> 210 us  [the longest x1 111 us: body(): grads = lax.psum_scatter(grads, DP, scatter_dimension=0, tiled=False)]
    all_gather x0 -> x1, waiting for transfers between devices: none -> 110 us  [body(): gathered = lax.all_gather(payload, EXPERT, axis=0, tiled=False)]
    dot_general x12 -> x0, matrix products: 41.6 us -> none  [the longest x1 6.83 us: body(): jnp.einsum('secd,efd->secf', grad_rows, down_matrix, preferred_element_ty...]
    pallas_call x0 -> x2, Pallas kernels: none -> 39.7 us  [the longest x1 37.6 us: run_experts(): pl.pallas_call(functools.partial(expert_kernel, cap=cap), grid=(mine,), o...]
    gather x9 -> x0, local copies, waits for them, and re-layouts: 39.5 us -> none  [the longest x2 15.5 us: fill_slots(): picked = jnp.take(source_rows, jnp.maximum(sources, 0) // divisor, axis=0)]
  transfers between devices with their start and end apart: 6 -> 4, of which waited for: 4 -> 4; matrix products, arithmetic and copies ran while one was open for 9% -> 1% of each run, Pallas kernels for 0% -> 0%
where the time goes in v1:
time: 634 us
  waiting for transfers between devices  573 us (90%)
  Pallas kernels  39.7 us (6%)
  between operations  13.8 us (2%)
  local copies, waits for them, and re-layouts  6.41 us (1%)
    psum x1, waiting for transfers between devices, body(): router_grad = lax.psum(router_part, ALL).T  252 us
    reduce_scatter x1, waiting for transfers between devices, body(): grads = lax.psum_scatter(grads, DP, scatter_dimension=0, tiled=False)  111 us
    all_gather x1, waiting for transfers between devices, body(): gathered = lax.all_gather(payload, EXPERT, axis=0, tiled=False)  110 us
    reduce_scatter x1, waiting for transfers between devices, body(): out = lax.psum_scatter(out, EXPERT, scatter_dimension=0, tiled=False)  99.2 us
    pallas_call x1, Pallas kernels, run_experts(): pl.pallas_call(functools.partial(expert_kernel, cap=cap), grid=(mine,), o...  37.6 us
  transfers between devices with their start and end apart: 4, of which 4 were waited for; matrix products, arithmetic and copies ran while one was open for 1% of the time, Pallas kernels for 0%

profile of v1, /device:TPU:2, one launch (start us, length us, event | category | flops | bytes accessed | tf_op | source)
XLA Modules:
  0.0 634.3 jit_solution(1331984410084852934)
XLA Ops:
  7.2 0.0 all-gather.3.cloned.1.call-start
  7.2 2.1 shard_map.118
  9.4 0.0 all-gather.3.cloned.1.call-update
  9.4 0.0 reduce-scatter.5.cloned.1.call-start
  9.4 109.6 %all-gather.3.cloned.1.call-done = bf16[4352,1024]{1,0:T(8,128)(2,1)} async-done(((bf16[272,1024]{1,0:T(8,128)(2,1)}), bf16[4352,1024]{1,0:T(8,128)(2,1)}) %all-gather.3.cloned.1.call-update) | async-done | bytes 8912912 | tf_op jit(solution)/shard_map/all_gather | solution.py:285
  119.1 37.6 %shard_map.119 = (bf16[16,256,1024]{2,1,0:T(8,128)(2,1)}, bf16[16,288,1024]{2,1,0:T(8,128)(2,1)}, f32[64,1024]{1,0:T(8,128)}) custom-call(s32[1]{0:T(128)} %bitcast.first, bf16[16,272,1024]{2,1,0:T(8,128)(2,1)} %bitcast.27, bf16[4,384,1024]{2,1,0:T(8,128)(2,1)} %gate.1, bf16[4,384,1024]{2,1,0:T(8,128)(2,1)} %up.1, bf16[4,384,1024]{2,1,0:T(8,128)(2,1)} %down.1, ...), custom_call_target="tpu_custom_call" | custom-call | flops 16000000000 | bytes 33554432 | tf_op jit(solution)/shard_map/pallas_call | solution.py:231
  156.7 0.0 reduce-scatter.5.cloned.1.call-update
  156.7 0.0 reduce-scatter.3.cloned.1.call-start
  156.7 0.7 reduce-scatter.3.cloned.1.call-update
  157.4 0.0 all-reduce.2.cloned.1.call-start
  157.5 0.5 all-reduce.2.cloned.1.call-update
  158.0 111.1 %reduce-scatter.5.cloned.1.call-done = bf16[1,288,1024]{2,1,0:T(8,128)(2,1)} async-done(((bf16[16,288,1024]{2,1,0:T(8,128)(2,1)}), bf16[1,288,1024]{2,1,0:T(8,128)(2,1)}) %reduce-scatter.5.cloned.1.call-update) | async-done | bytes 589840 | tf_op jit(solution)/shard_map/reduce_scatter | solution.py:291
  269.1 0.9 slice.39
  270.1 0.8 convert.3
  270.9 1.0 slice.36
  271.9 0.1 convert.2
  272.0 0.9 slice_bitcast_fusion
  272.9 99.2 %reduce-scatter.3.cloned.1.call-done = bf16[1,256,1024]{2,1,0:T(8,128)(2,1)} async-done(((bf16[16,256,1024]{2,1,0:T(8,128)(2,1)}), bf16[1,256,1024]{2,1,0:T(8,128)(2,1)}) %reduce-scatter.3.cloned.1.call-update) | async-done | bytes 524304 | tf_op jit(solution)/shard_map/reduce_scatter | solution.py:292
  372.1 1.9 slice_bitcast_fusion.2
  374.0 252.1 %all-reduce.2.cloned.1.call-done = f32[1024,64]{0,1:T(8,128)} async-done(((f32[1024,64]{0,1:T(8,128)}), f32[1024,64]{0,1:T(8,128)}) %all-reduce.2.cloned.1.call-update) | async-done | bytes 262160 | tf_op jit(solution)/shard_map/psum | solution.py:290
  626.1 1.7 copy.18
Async XLA Ops:
  7.2 111.9 %all-gather.3.cloned.1.call-start = ((), (), s32[]{:S(2)}) async-start(), calls=%async_computation.5 | async-start | bytes 9469952 | tf_op jit(solution)/shard_map/all_gather | solution.py:285
  9.4 259.8 %reduce-scatter.5.cloned.1.call-start = ((), (), s32[]{:S(2)}) async-start(), calls=%async_computation.4 | async-start | bytes 10027008 | tf_op jit(solution)/shard_map/reduce_scatter | solution.py:291
  156.7 215.4 %reduce-scatter.3.cloned.1.call-start = ((), (), s32[]{:S(2)}) async-start(), calls=%async_computation.2 | async-start | bytes 8912896 | tf_op jit(solution)/shard_map/reduce_scatter | solution.py:292
  157.4 468.7 %all-reduce.2.cloned.1.call-start = ((), (), s32[]{:S(2)}) async-start(), calls=%async_computation.3 | async-start | bytes 524288 | tf_op jit(solution)/shard_map/psum | solution.py:290
Sparse Core Ops, SparseCore 0:
  9.8 109.2 all-gather.2
  156.8 112.2 reduce-scatter.4
  271.7 100.3 reduce-scatter.2
  378.0 248.0 all-reduce.1

commit v2 on v1

--- a/solution.py
+++ b/solution.py
@@ -169,7 +169,7 @@
     piece = gate_grad.shape[0] // chunks
     for d in range(chunks):
         cut = slice(d * piece, d * piece + piece)
-        grads[d, pl.ds(pl.multiple_of(e * 2 * piece, 2 * piece), 2 * piece), :] = jnp.concatenate(
+        grads[(d % 2) * (chunks // 2) + d // 2, pl.ds(pl.multiple_of(e * 2 * piece, 2 * piece), 2 * piece), :] = jnp.concatenate(
             [gate_grad[cut], up_grad[cut]], axis=0
         ).astype(BF)
     down_grad = tn(scaled, u)
@@ -183,7 +183,7 @@
         base = mine * 2 * piece + (e // 2) * 2 * piece
         for d in range(chunks):
             cut = slice(d * piece, d * piece + piece)
-            grads[d, pl.ds(pl.multiple_of(base, 2 * piece), 2 * piece), :] = jnp.concatenate(
+            grads[(d % 2) * (chunks // 2) + d // 2, pl.ds(pl.multiple_of(base, 2 * piece), 2 * piece), :] = jnp.concatenate(
                 [down_kept[cut], down_grad[cut]], axis=0
             ).astype(BF)
 
@@ -218,6 +218,16 @@
             out[2 * p, rows : 2 * rows] = back[0:rows]
             out[2 * p + 1, rows : 2 * rows] = back[rows:]
 
+        half = width // 2
+        end = grads.shape[1] - 16
+        for d in range(chunks):
+            part = router_part[8 * (d // 2) : 8 * (d // 2) + 8, half * (d % 2) : half * (d % 2 + 1)]
+            high = part.astype(BF).astype(F32)
+            split = jnp.concatenate([high, part - high], axis=1)
+            grads[(d % 2) * (chunks // 2) + d // 2, end : end + 16] = jnp.concatenate(
+                [split, jnp.zeros_like(split)], axis=0
+            ).astype(BF)
+
 
 def run_experts(first, payload, gate, up, down, router, cap, chunks):
     sources, payload_rows, width = payload.shape
@@ -227,14 +237,13 @@
     pairs, slots, total = sources // 2, 2 * mine * cap, sources * cap
     whole = functools.partial(pl.BlockSpec, pipeline_mode=pl.Buffered(1))
     one = lambda: pl.BlockSpec((1, hidden, width), lambda e: (e, 0, 0))
-    grad_rows = 3 * mine * hidden // chunks
+    grad_rows = 3 * mine * hidden // chunks + 16
     return pl.pallas_call(
         functools.partial(expert_kernel, cap=cap),
         grid=(mine,),
         out_shape=(
             jax.ShapeDtypeStruct((sources, 2 * rows, width), BF),
             jax.ShapeDtypeStruct((chunks, grad_rows, width), BF),
-            jax.ShapeDtypeStruct((experts, width), F32),
         ),
         in_specs=[
             pl.BlockSpec(memory_space=pltpu.SMEM),
@@ -247,9 +256,9 @@
         out_specs=(
             whole((sources, 2 * rows, width), lambda e: (0, 0, 0)),
             whole((chunks, grad_rows, width), lambda e: (0, 0, 0)),
-            whole((experts, width), lambda e: (0, 0)),
         ),
         scratch_shapes=[
+            pltpu.VMEM((experts, width), F32),
             pltpu.VMEM((mine, total, width), BF),
             pltpu.VMEM((mine, total, width), BF),
             pltpu.VMEM((pairs, slots, 2 * rows), BF),
@@ -269,6 +278,16 @@
     )(first, payload, gate, up, down, router)
 
 
+def swap(value, axis, step):
+    size = lax.axis_size(axis)
+    return lax.ppermute(value, axis, [(i, i ^ step) for i in range(size)])
+
+
+def joined(value):
+    half = value.shape[-1] // 2
+    return value[..., 0:half].astype(F32) + value[..., half:].astype(F32)
+
+
 def body(tokens, expert_ids, upstream, router_weight, gate_matrix, up_matrix, down_matrix):
     rows, width = tokens.shape
     top = expert_ids.shape[1]
@@ -284,15 +303,31 @@
     )(tokens, expert_ids.T, upstream, router)
     gathered = lax.all_gather(payload, EXPERT, axis=0, tiled=False)
     first = (lax.axis_index(EXPERT) * mine).reshape(1).astype(jnp.int32)
-    out, grads, router_part = run_experts(
+    out, grads = run_experts(
         first, gathered, gate_matrix, up_matrix, down_matrix, router, cap, groups
     )
-    router_grad = lax.psum(router_part, ALL).T
-    grads = lax.psum_scatter(grads, DP, scatter_dimension=0, tiled=False)
     out = lax.psum_scatter(out, EXPERT, scatter_dimension=0, tiled=False)
     piece = hidden // groups
-    both = grads[0 : 2 * mine * piece].astype(F32).reshape(mine, 2, piece, width)
-    down_grad = grads[2 * mine * piece :].astype(F32).reshape(mine, piece, width)
+    end = 3 * mine * piece
+    core = lax.axis_index("core")
+    both = grads.reshape(2, groups // 2, end + 16, width)
+    theirs = swap(lax.dynamic_index_in_dim(both, 1 - core, 0, keepdims=False), "core", 1)
+    ours = lax.dynamic_index_in_dim(both, core, 0, keepdims=False)
+    sums = (ours[:, 0:end].astype(F32) + theirs[:, 0:end].astype(F32)).astype(BF)
+    part = joined(ours[:, end : end + 8]) + joined(theirs[:, end : end + 8])
+    high = lax.reduce_precision(part, 8, 7)
+    split = jnp.concatenate([high, part - high], axis=2).astype(BF)
+    send = jnp.concatenate([sums, split, jnp.zeros_like(split)], axis=1)
+    got = lax.all_to_all(send, ("x", "yh"), split_axis=0, concat_axis=0, tiled=True)
+    total = jnp.sum(got[:, 0:end].astype(F32), axis=0)
+    both = total[0 : 2 * mine * piece].reshape(mine, 2, piece, width)
+    down_grad = total[2 * mine * piece :].reshape(mine, piece, width)
+    part = jnp.sum(joined(got[:, end : end + 8]), axis=0)
+    for axis, step in (("yl", 1), ("z", 1), ("z", 2), ("z", 4)):
+        part = part + swap(part, axis, step)
+    parts = lax.all_gather(part, DP, axis=0, tiled=False)
+    parts = parts.reshape(groups // 2, 2, 8, width // 2).transpose(0, 2, 1, 3)
+    router_grad = parts.reshape(experts, width).T
     return out[0:rows], out[rows:], router_grad, both[:, 0], both[:, 1], down_grad
 
 

time: 634 us -> 363 us (0.57)
  waiting for transfers between devices: 573 us -> 135 us
  blocking collectives: 0 us -> 152 us
    psum x1 -> x0, waiting for transfers between devices: 252 us -> none  [body(): router_grad = lax.psum(router_part, ALL).T]
    all_to_all x0 -> x1, blocking collectives: none -> 132 us  [body(): lax.all_to_all(send, ('x', 'yh'), split_axis=0, concat_axis=0, tiled=True)]
    reduce_scatter x1 -> x0, waiting for transfers between devices: 111 us -> none  [body(): grads = lax.psum_scatter(grads, DP, scatter_dimension=0, tiled=False)]
    reduce_scatter x1, waiting for transfers between devices: 99.2 us -> 0.01 us  [body(): out = lax.psum_scatter(out, EXPERT, scatter_dimension=0, tiled=False)]
    ppermute x0 -> x5, waiting for transfers between devices: none -> 24.9 us  [swap(): return lax.ppermute(value, axis, [(i, i ^ step) for i in range(size)])]
    all_gather x0 -> x1, blocking collectives: none -> 20.1 us  [body(): parts = lax.all_gather(part, DP, axis=0, tiled=False)]
    squeeze x0 -> x1, local copies, waits for them, and re-layouts: none -> 7.43 us  [body(): ours = lax.dynamic_index_in_dim(both, core, 0, keepdims=False)]
  transfers between devices with their start and end apart: 4 -> 7, of which waited for: 4 -> 6; matrix products, arithmetic and copies ran while one was open for 1% -> 4% of each run, Pallas kernels for 0% -> 0%
where the time goes in v2:
time: 363 us; the launch traced here: 359 us
  blocking collectives  152 us (42%)
  waiting for transfers between devices  135 us (37%)
  Pallas kernels  39.8 us (11%)
  between operations  14.1 us (4%)
  local copies, waits for them, and re-layouts  11.8 us (3%)
  other arithmetic  6.02 us (2%)
    all_to_all x1, blocking collectives, body(): lax.all_to_all(send, ('x', 'yh'), split_axis=0, concat_axis=0, tiled=True)  132 us
    all_gather x1, waiting for transfers between devices, body(): gathered = lax.all_gather(payload, EXPERT, axis=0, tiled=False)  110 us
    pallas_call x1, Pallas kernels, run_experts(): pl.pallas_call(functools.partial(expert_kernel, cap=cap), grid=(mine,), o...  37.6 us
    ppermute x5, waiting for transfers between devices, swap(): return lax.ppermute(value, axis, [(i, i ^ step) for i in range(size)])  24.9 us
    all_gather x1, blocking collectives, body(): parts = lax.all_gather(part, DP, axis=0, tiled=False)  20.1 us
    squeeze x1, local copies, waits for them, and re-layouts, body(): ours = lax.dynamic_index_in_dim(both, core, 0, keepdims=False)  7.43 us
  transfers between devices with their start and end apart: 7, of which 6 were waited for; matrix products, arithmetic and copies ran while one was open for 4% of the time, Pallas kernels for 0%

profile of v2, /device:TPU:2, one launch (start us, length us, event | category | flops | bytes accessed | tf_op | source)
XLA Modules:
  0.0 359.0 jit_solution(15052574726966697734)
XLA Ops:
  7.2 0.0 all-gather.4.cloned.1.call-start
  7.2 2.1 shard_map.118
  9.3 0.0 all-gather.4.cloned.1.call-update
  9.4 0.0 reduce-scatter.2.cloned.1.call-start
  9.4 109.6 %all-gather.4.cloned.1.call-done = bf16[4352,1024]{1,0:T(8,128)(2,1)} async-done(((bf16[272,1024]{1,0:T(8,128)(2,1)}), bf16[4352,1024]{1,0:T(8,128)(2,1)}) %all-gather.4.cloned.1.call-update) | async-done | bytes 8912912 | tf_op jit(solution)/shard_map/all_gather | solution.py:304
  119.1 37.6 %shard_map.119 = (bf16[16,256,1024]{2,1,0:T(8,128)(2,1)}, bf16[16,304,1024]{2,1,0:T(8,128)(2,1)}) custom-call(s32[1]{0:T(128)} %bitcast.first, bf16[16,272,1024]{2,1,0:T(8,128)(2,1)} %bitcast.33, bf16[4,384,1024]{2,1,0:T(8,128)(2,1)} %gate.1, bf16[4,384,1024]{2,1,0:T(8,128)(2,1)} %up.1, bf16[4,384,1024]{2,1,0:T(8,128)(2,1)} %down.1, bf16[64,1024]{1,0:T(8,128)(2,1)} %bitcast.31), custom_call_target="tpu_custom_call" | custom-call | flops 16000000000 | bytes 33554432 | tf_op jit(solution)/shard_map/pallas_call | solution.py:241
  156.7 0.0 reduce-scatter.2.cloned.1.call-update
  156.7 7.4 %dynamic-slice_bitcast_fusion.1 = (bf16[8,304,1024]{2,1,0:T(8,128)(2,1)S(1)}, bf16[8,304,1024]{2,1,0:T(8,128)(2,1)}) fusion(bf16[2,8,304,1024]{3,2,1,0:T(8,128)(2,1)} %bitcast.26, s32[]{:T(128)S(6)} %select_n.7, s32[]{:T(128)S(6)} %select_n.8), kind=kLoop, calls=%fused_computation.4 | loop fusion | bytes 19922952 | tf_op jit(solution)/shard_map/jit(dynamic_index_in_dim)/squeeze | solution.py:315
  164.2 0.0 collective-permute-start
  164.2 0.1 pad.3.clone
  164.2 8.4 %collective-permute-done = bf16[8,304,1024]{2,1,0:T(8,128)(2,1)S(1)} collective-permute-done((bf16[8,304,1024]{2,1,0:T(8,128)(2,1)}, bf16[8,304,1024]{2,1,0:T(8,128)(2,1)S(1)}, u32[]{:S(2)}, u32[]{:S(2)}) %collective-permute-start) | collective-permute-done | bytes 4980768 | tf_op jit(solution)/shard_map/ppermute | solution.py:283
  172.7 2.5 add_convert_fusion
  175.2 2.4 maximum_maximum_fusion
  177.6 131.9 %all_to_all.5 = bf16[8,304,1024]{2,1,0:T(8,128)(2,1)S(1)} all-to-all(bf16[8,304,1024]{2,1,0:T(8,128)(2,1)S(1)} %maximum_maximum_fusion), channel_id=1, replica_groups=mesh['x'=4,'yh'=2,'core'=2,'yl'=2,'z'=8] {'x','yh'}, dimensions={0} | all-to-all | bytes 9961472 | tf_op jit(solution)/shard_map/all_to_all | solution.py:321
  309.5 0.7 collective-permute-start.1
  310.2 3.2 collective-permute-done.1
  313.3 0.0 collective-permute-start.2
  313.4 3.7 %collective-permute-done.2 = f32[8,512]{1,0:T(8,128)S(1)} collective-permute-done((f32[8,512]{1,0:T(8,128)S(1)}, f32[8,512]{1,0:T(8,128)S(1)}, u32[]{:S(2)}, u32[]{:S(2)}) %collective-permute-start.2) | collective-permute-done | bytes 16416 | tf_op jit(solution)/shard_map/ppermute | solution.py:283
  317.1 0.0 collective-permute-start.3
  317.1 1.0 convert_reduce_fusion
  318.1 0.1 slice.88
  318.2 3.6 collective-permute-done.3
  321.7 0.0 collective-permute-start.4
  321.7 0.9 slice_bitcast_fusion
  322.7 0.8 slice.91
  323.4 6.0 %collective-permute-done.4 = f32[8,512]{1,0:T(8,128)S(1)} collective-permute-done((f32[8,512]{1,0:T(8,128)S(1)}, f32[8,512]{1,0:T(8,128)S(1)}, u32[]{:S(2)}, u32[]{:S(2)}) %collective-permute-start.4) | collective-permute-done | bytes 16416 | tf_op jit(solution)/shard_map/ppermute | solution.py:283
  329.5 20.1 %all-gather.1 = f32[128,512]{1,0:T(8,128)S(1)} all-gather(f32[8,512]{1,0:T(8,128)S(1)} %add.51), channel_id=3, replica_groups=mesh['x'=4,'yh'=2,'core'=2,'yl'=2,'z'=8] {'x','yh','core'}, dimensions={0}, use_global_device_ids=true | all-gather | bytes 278528 | tf_op jit(solution)/shard_map/all_gather | solution.py:328
  349.6 0.0 reduce-scatter.2.cloned.1.call-done
  349.6 1.9 slice_bitcast_fusion.2
  351.5 0.7 copy.14
  (7 shorter events, 0.1 us)
Async XLA Ops:
  7.2 111.9 %all-gather.4.cloned.1.call-start = ((), (), s32[]{:S(2)}) async-start(), calls=%async_computation.3 | async-start | bytes 9469952 | tf_op jit(solution)/shard_map/all_gather | solution.py:304
  9.4 340.3 %reduce-scatter.2.cloned.1.call-start = ((), (), s32[]{:S(2)}) async-start(), calls=%async_computation.2 | async-start | bytes 8912896 | tf_op jit(solution)/shard_map/reduce_scatter | solution.py:309
  164.2 8.5 %collective-permute-start = (bf16[8,304,1024]{2,1,0:T(8,128)(2,1)}, bf16[8,304,1024]{2,1,0:T(8,128)(2,1)S(1)}, u32[]{:S(2)}, u32[]{:S(2)}) collective-permute-start(bf16[8,304,1024]{2,1,0:T(8,128)(2,1)} %get-tuple-element.13), channel_id=1, source_target_pairs={{0,16},{16,0},{1,17},{17,1},{2,18},{18,2},{3,19},{19,3},{4,20},{20... | collective-permute-start | bytes 14942216 | tf_op jit(solution)/shard_map/ppermute | solution.py:283
  309.5 3.8 %collective-permute-start.1 = (f32[8,512]{1,0:T(8,128)S(1)}, f32[8,512]{1,0:T(8,128)S(1)}, u32[]{:S(2)}, u32[]{:S(2)}) collective-permute-start(f32[8,512]{1,0:T(8,128)S(1)} %add_reduce_fusion), channel_id=1, source_target_pairs={{0,8},{8,0},{1,9},{9,1},{2,10},{10,2},{3,11},{11,3},{4,12},{12,4},... | collective-permute-start | bytes 49160 | tf_op jit(solution)/shard_map/ppermute | solution.py:283
  313.3 3.7 %collective-permute-start.2 = (f32[8,512]{1,0:T(8,128)S(1)}, f32[8,512]{1,0:T(8,128)S(1)}, u32[]{:S(2)}, u32[]{:S(2)}) collective-permute-start(f32[8,512]{1,0:T(8,128)S(1)} %add.48), channel_id=1, source_target_pairs={{0,1},{1,0},{2,3},{3,2},{4,5},{5,4},{6,7},{7,6},{8,9},{9,8},{10,11... | collective-permute-start | bytes 49160 | tf_op jit(solution)/shard_map/ppermute | solution.py:283
  317.1 4.6 %collective-permute-start.3 = (f32[8,512]{1,0:T(8,128)S(1)}, f32[8,512]{1,0:T(8,128)S(1)}, u32[]{:S(2)}, u32[]{:S(2)}) collective-permute-start(f32[8,512]{1,0:T(8,128)S(1)} %add.49), channel_id=1, source_target_pairs={{0,2},{1,3},{2,0},{3,1},{4,6},{5,7},{6,4},{7,5},{8,10},{9,11},{10,... | collective-permute-start | bytes 49160 | tf_op jit(solution)/shard_map/ppermute | solution.py:283
  321.7 7.7 %collective-permute-start.4 = (f32[8,512]{1,0:T(8,128)S(1)}, f32[8,512]{1,0:T(8,128)S(1)}, u32[]{:S(2)}, u32[]{:S(2)}) collective-permute-start(f32[8,512]{1,0:T(8,128)S(1)} %add.50), channel_id=1, source_target_pairs={{0,4},{1,5},{2,6},{3,7},{4,0},{5,1},{6,2},{7,3},{8,12},{9,13},{10,... | collective-permute-start | bytes 49160 | tf_op jit(solution)/shard_map/ppermute | solution.py:283
Sparse Core Ops, SparseCore 0:
  9.8 109.2 all-gather.3
  156.8 138.9 reduce-scatter.1
